TPU v7x, 32 devices: a whole 2x2x4 slice. The times are simulated.
32 devices in a mesh: sub: 8 (over y, x, core), col: 4 (over z).
Axes of the slice: x: 2, y: 2, z: 4, core: 2. Of those that a mesh axis runs over, the one named last changes fastest.
Arguments:
- perm: float32 [512, 512, 128], P('sub', 'col'), may hold values from 0.1 to 10
- accum: float32 [512, 512, 128], P('sub', 'col'), may hold values from 0.05 to 2
- rhs: float32 [512, 512, 128], P('sub', 'col'), may hold values from -24 to 24
- depth_x: int32 [16, 512], P('sub', 'col'), may hold values from 0 to 4, as said below
- depth_y: int32 [512, 8], P('sub', 'col'), may hold values from 0 to 4, as said below
Outputs:
- pressure: float32 [512, 512, 128], P('sub', 'col')
Inputs may be any that keep to these rules, and one draw needn't show every extreme that they name: Both sides of one interface share its depth: depth_x[2 s + 1, j] = depth_x[2 s + 2, j] and depth_y[i, 2 c + 1] = depth_y[i, 2 c + 2]; faces on the grid's boundary have depth 0; the depth 4 occurs. `depth_y`: as for depth_x, along the second dimension.
All inputs are finite; a program needn't handle non-finite values.
Results may differ from a plain program's by a relative error of at most 0.0003.
Values sent between devices are 32-bit elements; how exact they have to be, the bound alone decides.
A program may use at most 192 MiB of HBM per device.

v0:
```python
import jax
import jax.numpy as jnp
from jax import lax
from jax.sharding import PartitionSpec as P

OVL = 4
SWEEPS = 3
ITERS = 2


VERTICAL = 0.1


def padded_2(block, sides, width):
    for axis, dim in sides:
        count = lax.axis_size(axis)
        forward = [(i, i + 1) for i in range(count - 1)]
        backward = [(target, source) for source, target in forward]
        low = lax.ppermute(
            lax.slice_in_dim(block, block.shape[dim] - width, None, axis=dim), axis, forward
        )
        high = lax.ppermute(lax.slice_in_dim(block, 0, width, axis=dim), axis, backward)
        block = jnp.concatenate([low, block, high], axis=dim)
    return block


def harmonic(first_perm, second_perm):
    return 2.0 * first_perm * second_perm / (first_perm + second_perm)


def coefficients(perm_padded, accum_centre, inside_x, inside_y):
    inside = inside_x[:, None, None] & inside_y[None, :, None]
    perm_safe = jnp.where(inside, perm_padded, 1.0)
    across_x = harmonic(perm_safe[:-1, 1:-1], perm_safe[1:, 1:-1])
    open_x = (inside_x[:-1] & inside_x[1:])[:, None, None]
    across_x = jnp.where(open_x, across_x, 0.0)
    across_y = harmonic(perm_safe[1:-1, :-1], perm_safe[1:-1, 1:])
    open_y = (inside_y[:-1] & inside_y[1:])[None, :, None]
    across_y = jnp.where(open_y, across_y, 0.0)
    centre = perm_safe[1:-1, 1:-1]
    upward = VERTICAL * harmonic(centre[:, :, :-1], centre[:, :, 1:])
    bottom = jnp.zeros_like(centre[:, :, :1])
    lower_z = jnp.concatenate([bottom, upward], axis=2)
    upper_z = jnp.concatenate([upward, bottom], axis=2)
    lower_x = across_x[:-1]
    upper_x = across_x[1:]
    lower_y = across_y[:, :-1]
    upper_y = across_y[:, 1:]
    diagonal = accum_centre + lower_x + upper_x + lower_y + upper_y + lower_z + upper_z
    return (diagonal, lower_x, upper_x, lower_y, upper_y, lower_z, upper_z)


def neighbour_sum(padded, coeffs):
    diagonal, lower_x, upper_x, lower_y, upper_y, lower_z, upper_z = coeffs
    centre = padded[1:-1, 1:-1]
    bottom = jnp.zeros_like(centre[:, :, :1])
    below = jnp.concatenate([bottom, centre[:, :, :-1]], axis=2)
    above = jnp.concatenate([centre[:, :, 1:], bottom], axis=2)
    total = lower_x * padded[:-2, 1:-1] + upper_x * padded[2:, 1:-1]
    total = total + lower_y * padded[1:-1, :-2] + upper_y * padded[1:-1, 2:]
    return total + lower_z * below + upper_z * above


def operate(padded, coeffs):
    return coeffs[0] * padded[1:-1, 1:-1] - neighbour_sum(padded, coeffs)


def membership(depth_lo_hi_x, depth_lo_hi_y, inside_x, inside_y, block_x, block_y, margin):
    row_ids = jnp.arange(block_x + 2 * margin, dtype=jnp.int32)[:, None]
    column_ids = jnp.arange(block_y + 2 * margin, dtype=jnp.int32)[None, :]
    in_rows = (row_ids >= margin) & (row_ids < margin + block_x)
    in_columns = (column_ids >= margin) & (column_ids < margin + block_y)
    low_x = jnp.pad(depth_lo_hi_x[0], (margin, margin))[None, :]
    high_x = jnp.pad(depth_lo_hi_x[1], (margin, margin))[None, :]
    low_y = jnp.pad(depth_lo_hi_y[:, 0], (margin, margin))[:, None]
    high_y = jnp.pad(depth_lo_hi_y[:, 1], (margin, margin))[:, None]
    member = in_rows & in_columns
    member = member | (row_ids < margin) & in_columns & (margin - 1 - row_ids < low_x)
    member = member | (row_ids >= margin + block_x) & in_columns & (
        row_ids - margin - block_x < high_x
    )
    member = member | (column_ids < margin) & in_rows & (margin - 1 - column_ids < low_y)
    member = member | (column_ids >= margin + block_y) & in_rows & (
        column_ids - margin - block_y < high_y
    )
    return member & inside_x[:, None] & inside_y[None, :]


def coverage_count(depth_lo_hi_x, depth_lo_hi_y, block_x, block_y):
    row_ids = jnp.arange(block_x, dtype=jnp.int32)[:, None]
    column_ids = jnp.arange(block_y, dtype=jnp.int32)[None, :]
    hits = (row_ids < depth_lo_hi_x[0][None, :]).astype(jnp.float32)
    hits = hits + (block_x - 1 - row_ids < depth_lo_hi_x[1][None, :]).astype(jnp.float32)
    hits = hits + (column_ids < depth_lo_hi_y[:, 0][:, None]).astype(jnp.float32)
    hits = hits + (block_y - 1 - column_ids < depth_lo_hi_y[:, 1][:, None]).astype(jnp.float32)
    return 1.0 + hits


def local_solve(resid_ext, coeffs, diag_safe, member_cells):
    correction = jnp.zeros_like(resid_ext)
    for sweep_index in range(SWEEPS):
        padded = jnp.pad(correction, ((1, 1), (1, 1), (0, 0)))
        correction = jnp.where(
            member_cells, (resid_ext + neighbour_sum(padded, coeffs)) / diag_safe, 0.0
        )
    return correction


def send_back(correction, block_x, block_y, margin):
    rim_x = jnp.concatenate(
        [
            correction[:margin, margin : margin + block_y],
            correction[margin + block_x :, margin : margin + block_y],
        ],
        axis=0,
    )
    arrived_x = padded_2(rim_x, (("sub", 0),), margin)
    rim_y = jnp.concatenate(
        [
            correction[margin : margin + block_x, :margin],
            correction[margin : margin + block_x, margin + block_y :],
        ],
        axis=1,
    )
    arrived_y = padded_2(rim_y, (("col", 1),), margin)
    owned = correction[margin : margin + block_x, margin : margin + block_y]
    owned = owned + jnp.pad(arrived_x[:margin], ((0, block_x - margin), (0, 0), (0, 0)))
    owned = owned + jnp.pad(arrived_x[3 * margin :], ((block_x - margin, 0), (0, 0), (0, 0)))
    owned = owned + jnp.pad(arrived_y[:, :margin], ((0, 0), (0, block_y - margin), (0, 0)))
    owned = owned + jnp.pad(arrived_y[:, 3 * margin :], ((0, 0), (block_y - margin, 0), (0, 0)))
    return owned


def shards(perm, accum, rhs, depth_x, depth_y):
    block_x, block_y, layers = perm.shape
    margin = OVL
    sub_index = lax.axis_index("sub")
    col_index = lax.axis_index("col")
    total_x = block_x * lax.axis_size("sub")
    total_y = block_y * lax.axis_size("col")
    row_global = (
        sub_index * block_x - (margin + 1) + jnp.arange(block_x + 2 * margin + 2, dtype=jnp.int32)
    )
    column_global = (
        col_index * block_y - (margin + 1) + jnp.arange(block_y + 2 * margin + 2, dtype=jnp.int32)
    )
    inside_x = (row_global >= 0) & (row_global < total_x)
    inside_y = (column_global >= 0) & (column_global < total_y)
    widened = padded_2(jnp.stack([perm, accum]), (("sub", 1), ("col", 2)), margin + 1)
    coeffs = coefficients(widened[0], widened[1, 1:-1, 1:-1], inside_x, inside_y)
    own_coeffs = tuple(
        (part[margin : margin + block_x, margin : margin + block_y] for part in coeffs)
    )
    member = membership(depth_x, depth_y, inside_x[1:-1], inside_y[1:-1], block_x, block_y, margin)
    member_cells = member[:, :, None]
    diag_safe = jnp.where(member_cells, coeffs[0], 1.0)
    coverage = coverage_count(depth_x, depth_y, block_x, block_y)
    pressure = jnp.zeros_like(rhs)
    for iteration in range(ITERS):
        if iteration == 0:
            residual = rhs
        else:
            nearby = padded_2(pressure, (("sub", 0), ("col", 1)), 1)
            residual = rhs - operate(nearby, own_coeffs)
        resid_ext = padded_2(residual, (("sub", 0), ("col", 1)), margin)
        correction = local_solve(resid_ext, coeffs, diag_safe, member_cells)
        pressure = pressure + send_back(correction, block_x, block_y, margin) / coverage[:, :, None]
    return pressure


def solution(mesh):
    placed = (
        P("sub", "col", None),
        P("sub", "col", None),
        P("sub", "col", None),
        P("sub", "col"),
        P("sub", "col"),
    )
    return jax.shard_map(
        shards, mesh=mesh, in_specs=placed, out_specs=P("sub", "col", None), check_vma=False
    )
```

profile of v0, /device:TPU:4, one launch (start us, length us, event | category | flops | bytes accessed | tf_op | source)
XLA Modules:
  0.0 396.8 jit_solution(6817751244902856074)
XLA Ops:
  0.0 2.4 pad_maximum_fusion.13
  2.5 1.9 collective-permute-start.4
  4.4 4.5 %collective-permute-start.5 = (f32[2,5,128,128]{3,0,2,1:T(2,128)S(1)}, f32[2,5,128,128]{3,0,2,1:T(2,128)S(1)}, u32[]{:S(2)}, u32[]{:S(2)}) collective-permute-start(f32[2,5,128,128]{3,0,2,1:T(2,128)S(1)} %get-tuple-element.11), channel_id=1, source_target_pairs={{4,0},{8,4},{12,8},{16,12},{20,16},{24,20},{28,24},{5,1},{9,5},{13... | collective-permute-start | bytes 1966088 | tf_op jit(solution)/shard_map/ppermute | solution.py:22
  8.9 1.8 fusion.91
  10.7 1.9 collective-permute-start
  12.6 4.5 %collective-permute-start.1 = (f32[4,128,128]{2,1,0:T(8,128)}, f32[4,128,128]{2,1,0:T(8,128)}, u32[]{:S(2)}, u32[]{:S(2)}) collective-permute-start(f32[4,128,128]{2,1,0:T(8,128)} %get-tuple-element.40), channel_id=1, source_target_pairs={{4,0},{8,4},{12,8},{16,12},{20,16},{24,20},{28,24},{5,1},{9,5},{13... | collective-permute-start | bytes 786440 | tf_op jit(solution)/shard_map/ppermute | solution.py:22
  18.2 6.9 %collective-permute-done = f32[4,128,128]{2,1,0:T(8,128)S(1)} collective-permute-done((f32[4,128,128]{2,1,0:T(8,128)S(1)}, f32[4,128,128]{2,1,0:T(8,128)S(1)}, u32[]{:S(2)}, u32[]{:S(2)}) %collective-permute-start) | collective-permute-done | bytes 262176 | tf_op jit(solution)/shard_map/ppermute | solution.py:19
  26.8 1.8 pad_maximum_fusion.17
  28.7 3.8 collective-permute-start.6
  32.5 1.3 collective-permute-start.7
  35.3 5.2 %collective-permute-start.2 = (f32[72,4,128]{2,1,0:T(4,128)S(1)}, f32[72,4,128]{2,1,0:T(4,128)}, u32[]{:S(2)}, u32[]{:S(2)}) collective-permute-start(f32[72,4,128]{2,1,0:T(4,128)S(1)} %get-tuple-element.30), channel_id=1, source_target_pairs={{0,1},{1,2},{2,3},{4,5},{5,6},{6,7},{8,9},{9,10},{10,11},{12,13},{... | collective-permute-start | bytes 442376 | tf_op jit(solution)/shard_map/ppermute | solution.py:19
  40.5 1.5 collective-permute-start.3
  42.7 25.8 %pad_maximum_fusion = f32[2,74,138,128]{3,0,2,1:T(2,128)S(1)} fusion(f32[2,74,5,128]{3,0,2,1:T(2,128)S(1)} %collective-permute-done.7, f32[2,5,128,128]{3,0,2,1:T(2,128)} %copy-done.8, f32[1,64,128,128]{3,0,2,1:T(1,128)S(1)} %bitcast.19, f32[1,64,128,128]{3,0,2,1:T(1,128)S(1)} %bitcast.23, f32[2,5,128,128]{3,0,2,1:T(2,128)S(1)} %copy-done.7, ...), kind=kLoop, calls=%fused_computation.4 | loop fusion | flops 13071360 | bytes 20914176 | tf_op jit(solution)/shard_map/concatenate | solution.py:23
  68.6 3.9 slice.393
  72.4 2.1 fusion
  74.5 1.5 divide_select_fusion
  76.0 2.1 divide_select_fusion.1
  78.3 43.3 %pad_maximum_fusion.1 = f32[1,72,136,128]{3,0,2,1:T(1,128)} fusion(f32[2,74,5,128]{3,0,2,1:T(2,128)S(1)} %collective-permute-done.7, f32[2,74,5,128]{3,0,2,1:T(2,128)S(1)} %collective-permute-done.6, f32[2,5,128,128]{3,0,2,1:T(2,128)S(1)} %copy-done.9, f32[2,5,128,128]{3,0,2,1:T(2,128)S(1)} %copy-done.7, f32[1,64,128,128]{3,0,2,1:T(1,128)S(1)} %bitcast.20, ...), kind=kLoop, calls=%fused_computation.78 | loop fusion | flops 6266880 | bytes 15470592 | tf_op jit(solution)/shard_map/slice | solution.py:150
  121.6 4.1 %divide_multiply_fusion = f32[72,136,127]{2,1,0:T(8,128)} fusion(f32[74,138,128]{2,1,0:T(8,128)S(1)} %fusion), kind=kLoop, calls=%fused_computation.84 | loop fusion | flops 6217920 | bytes 14923008 | tf_op jit(solution)/shard_map/mul | solution.py:41
  125.7 2.6 slice.320
  128.4 24.6 %divide_select_fusion.3 = (f32[72,136,128]{2,1,0:T(8,128)}, f32[72,136,128]{2,1,0:T(8,128)}, f32[72,136,128]{2,1,0:T(8,128)}) fusion(pred[72,136]{1,0:T(8,128)(4,1)S(1)} %and_and_fusion, f32[72,4,128]{2,1,0:T(4,128)} %collective-permute-done.3, f32[72,128,128]{2,1,0:T(8,128)} %copy-done.4, f32[72,4,128]{2,1,0:T(4,128)} %collective-permute-done.2, ...), kind=kLoop, calls=%fused_computation.82 | loop fusion | flops 28827648 | bytes 55119680 | tf_op jit(solution)/shard_map/jit(_where)/select_n | solution.py:103
  152.9 9.1 %fusion.86 = (f32[72,136,127]{2,1,0:T(8,128)}, f32[72,136,127]{2,1,0:T(8,128)}) fusion(f32[72,136,128]{2,1,0:T(8,128)} %get-tuple-element.5), kind=kLoop, calls=%fused_computation.167 | loop fusion | bytes 19897344 | tf_op jit(solution)/shard_map/slice | solution.py:57
  162.1 21.6 %fusion.57 = f32[72,136,128]{2,1,0:T(8,128)} fusion(f32[72,136,127]{2,1,0:T(8,128)} %get-tuple-element.27, f32[72,136,127]{2,1,0:T(8,128)} %get-tuple-element.26, f32[72,136,128]{2,1,0:T(8,128)} %get-tuple-element.5, f32[72,137,128]{2,1,0:T(8,128)S(1)} %divide_select_fusion, f32[73,136,128]{2,1,0:T(8,128)S(1)} %divide_select_fusion.1, ...), kind=kLoop, calls=%fused_computation.88 | loop fusion | flops 21307392 | bytes 55040832 | tf_op jit(solution)/shard_map/jit(_where)/select_n | solution.py:103
  183.7 9.1 %fusion.85 = (f32[72,136,127]{2,1,0:T(8,128)}, f32[72,136,127]{2,1,0:T(8,128)}) fusion(f32[72,136,128]{2,1,0:T(8,128)} %fusion.57), kind=kLoop, calls=%fused_computation.166 | loop fusion | bytes 19897344 | tf_op jit(solution)/shard_map/slice | solution.py:57
  192.8 23.2 %fusion.56 = f32[72,136,128]{2,1,0:T(8,128)} fusion(f32[72,136,127]{2,1,0:T(8,128)} %get-tuple-element.25, f32[72,136,127]{2,1,0:T(8,128)} %get-tuple-element.24, f32[72,136,128]{2,1,0:T(8,128)} %fusion.57, f32[72,137,128]{2,1,0:T(8,128)S(1)} %divide_select_fusion, f32[73,136,128]{2,1,0:T(8,128)S(1)} %divide_select_fusion.1, ...), kind=kLoop, calls=%fused_computation.87 | loop fusion | flops 21307392 | bytes 55040832 | tf_op jit(solution)/shard_map/jit(_where)/select_n | solution.py:103
  217.0 1.9 collective-permute-start.8
  219.0 4.5 %collective-permute-start.9 = (f32[4,128,128]{2,1,0:T(8,128)S(1)}, f32[4,128,128]{2,1,0:T(8,128)S(1)}, u32[]{:S(2)}, u32[]{:S(2)}) collective-permute-start(f32[4,128,128]{2,1,0:T(8,128)S(1)} %get-tuple-element.21), channel_id=1, source_target_pairs={{4,0},{8,4},{12,8},{16,12},{20,16},{24,20},{28,24},{5,1},{9,5},{13... | collective-permute-start | bytes 786440 | tf_op jit(solution)/shard_map/ppermute | solution.py:22
  223.5 1.1 fusion.84
  224.6 4.1 %collective-permute-start.10 = (f32[64,4,128]{2,1,0:T(4,128)S(1)}, f32[64,4,128]{2,1,0:T(4,128)S(1)}, u32[]{:S(2)}, u32[]{:S(2)}) collective-permute-start(f32[64,4,128]{2,1,0:T(4,128)S(1)} %get-tuple-element.22), channel_id=1, source_target_pairs={{0,1},{1,2},{2,3},{4,5},{5,6},{6,7},{8,9},{9,10},{10,11},{12,13},{... | collective-permute-start | bytes 393224 | tf_op jit(solution)/shard_map/ppermute | solution.py:19
  228.7 1.3 collective-permute-start.11
  230.1 1.1 collective-permute-done.10
  231.2 4.4 %collective-permute-done.11 = f32[64,4,128]{2,1,0:T(4,128)S(1)} collective-permute-done((f32[64,4,128]{2,1,0:T(4,128)S(1)}, f32[64,4,128]{2,1,0:T(4,128)S(1)}, u32[]{:S(2)}, u32[]{:S(2)}) %collective-permute-start.11) | collective-permute-done | bytes 131104 | tf_op jit(solution)/shard_map/ppermute | solution.py:22
  235.6 3.7 fusion.77
  239.3 1.9 collective-permute-start.12
  241.2 4.5 %collective-permute-start.13 = (f32[1,128,128]{2,1,0:T(8,128)S(1)}, f32[1,128,128]{2,1,0:T(8,128)S(1)}, u32[]{:S(2)}, u32[]{:S(2)}) collective-permute-start(f32[1,128,128]{2,1,0:T(8,128)S(1)} %get-tuple-element.39), channel_id=1, source_target_pairs={{4,0},{8,4},{12,8},{16,12},{20,16},{24,20},{28,24},{5,1},{9,5},{13... | collective-permute-start | bytes 196616 | tf_op jit(solution)/shard_map/ppermute | solution.py:22
  245.8 1.9 collective-permute-done.13
  247.7 3.5 collective-permute-start.14
  251.2 1.6 collective-permute-start.15
  252.8 4.9 %fusion.89 = (f32[64,128,127]{2,1,0:T(8,128)}, f32[64,128,127]{2,1,0:T(8,128)}) fusion(f32[64,128,128]{2,1,0:T(8,128)S(1)} %fusion.77), kind=kLoop, calls=%fused_computation.170 | loop fusion | bytes 16646144 | tf_op jit(solution)/shard_map/slice | solution.py:57
  257.8 14.6 %fusion.68 = f32[64,128,128]{2,1,0:T(8,128)} fusion(f32[64,128,128]{2,1,0:T(8,128)} %param.7, f32[66,1,128]{2,1,0:T(1,128)S(1)} %collective-permute-done.15, f32[1,128,128]{2,1,0:T(8,128)S(1)} %collective-permute-done.13, f32[64,128,128]{2,1,0:T(8,128)S(1)} %fusion.77, f32[1,128,128]{2,1,0:T(8,128)S(1)} %collective-permute-done.12, ...), kind=kLoop, calls=%fused_computation.101 | loop fusion | flops 23068672 | bytes 47050496 | tf_op jit(solution)/shard_map/sub | solution.py:164
  272.4 1.2 fusion.88
  273.6 2.1 collective-permute-start.16
  275.7 4.5 %collective-permute-start.17 = (f32[4,128,128]{2,1,0:T(8,128)S(1)}, f32[4,128,128]{2,1,0:T(8,128)S(1)}, u32[]{:S(2)}, u32[]{:S(2)}) collective-permute-start(f32[4,128,128]{2,1,0:T(8,128)S(1)} %get-tuple-element.35), channel_id=1, source_target_pairs={{4,0},{8,4},{12,8},{16,12},{20,16},{24,20},{28,24},{5,1},{9,5},{13... | collective-permute-start | bytes 786440 | tf_op jit(solution)/shard_map/ppermute | solution.py:22
  280.2 2.5 collective-permute-done.16
  282.7 1.4 collective-permute-done.17
  284.1 1.2 pad_maximum_fusion.20
  285.3 4.6 %collective-permute-start.18 = (f32[72,4,128]{2,1,0:T(4,128)S(1)}, f32[72,4,128]{2,1,0:T(4,128)S(1)}, u32[]{:S(2)}, u32[]{:S(2)}) collective-permute-start(f32[72,4,128]{2,1,0:T(4,128)S(1)} %get-tuple-element.28), channel_id=1, source_target_pairs={{0,1},{1,2},{2,3},{4,5},{5,6},{6,7},{8,9},{9,10},{10,11},{12,13},{... | collective-permute-start | bytes 442376 | tf_op jit(solution)/shard_map/ppermute | solution.py:19
  289.8 1.3 collective-permute-start.19
  291.1 1.3 collective-permute-done.18
  292.5 4.4 %collective-permute-done.19 = f32[72,4,128]{2,1,0:T(4,128)S(1)} collective-permute-done((f32[72,4,128]{2,1,0:T(4,128)S(1)}, f32[72,4,128]{2,1,0:T(4,128)S(1)}, u32[]{:S(2)}, u32[]{:S(2)}) %collective-permute-start.19) | collective-permute-done | bytes 147488 | tf_op jit(solution)/shard_map/ppermute | solution.py:22
  297.5 9.7 %divide_select_fusion.2 = f32[72,136,128]{2,1,0:T(8,128)} fusion(f32[72,136,128]{2,1,0:T(8,128)} %get-tuple-element.7, f32[72,136,128]{2,1,0:T(8,128)} %get-tuple-element.6, pred[72,136]{1,0:T(8,128)(4,1)S(1)} %and_and_fusion, f32[72,4,128]{2,1,0:T(4,128)S(1)} %collective-permute-done.19, f32[4,128,128]{2,1,0:T(8,128)S(1)} %collective-permute-done.17, ...), kind=kLoop, calls=%fused_computation.81 | loop fusion | flops 10027008 | bytes 20063808 | tf_op jit(solution)/shard_map/jit(_where)/select_n | solution.py:103
  307.3 9.1 %fusion.82 = (f32[72,136,127]{2,1,0:T(8,128)}, f32[72,136,127]{2,1,0:T(8,128)}) fusion(f32[72,136,128]{2,1,0:T(8,128)} %divide_select_fusion.2), kind=kLoop, calls=%fused_computation.163 | loop fusion | bytes 19897344 | tf_op jit(solution)/shard_map/slice | solution.py:57
  316.3 23.2 %fusion.55 = f32[72,136,128]{2,1,0:T(8,128)} fusion(f32[72,136,127]{2,1,0:T(8,128)} %get-tuple-element.19, f32[72,136,127]{2,1,0:T(8,128)} %get-tuple-element.18, f32[72,136,128]{2,1,0:T(8,128)} %divide_select_fusion.2, f32[72,137,128]{2,1,0:T(8,128)S(1)} %divide_select_fusion, f32[73,136,128]{2,1,0:T(8,128)S(1)} %divide_select_fusion.1, ...), kind=kLoop, calls=%fused_computation.86 | loop fusion | flops 23814144 | bytes 55040832 | tf_op jit(solution)/shard_map/jit(_where)/select_n | solution.py:103
  339.5 9.1 %fusion.81 = (f32[72,136,127]{2,1,0:T(8,128)}, f32[72,136,127]{2,1,0:T(8,128)}) fusion(f32[72,136,128]{2,1,0:T(8,128)} %fusion.55), kind=kLoop, calls=%fused_computation.162 | loop fusion | bytes 19897344 | tf_op jit(solution)/shard_map/slice | solution.py:57
  348.6 23.4 %fusion.54 = f32[72,136,128]{2,1,0:T(8,128)} fusion(f32[72,136,127]{2,1,0:T(8,128)} %get-tuple-element.17, f32[72,136,127]{2,1,0:T(8,128)} %get-tuple-element.16, f32[72,136,128]{2,1,0:T(8,128)} %fusion.55, f32[72,137,128]{2,1,0:T(8,128)S(1)} %divide_select_fusion, f32[73,136,128]{2,1,0:T(8,128)S(1)} %divide_select_fusion.1, ...), kind=kLoop, calls=%fused_computation.85 | loop fusion | flops 23814144 | bytes 55040832 | tf_op jit(solution)/shard_map/jit(_where)/select_n | solution.py:103
  372.0 1.1 fusion.79
  373.1 1.9 collective-permute-start.20
  375.0 4.5 %collective-permute-start.21 = (f32[4,128,128]{2,1,0:T(8,128)S(1)}, f32[4,128,128]{2,1,0:T(8,128)S(1)}, u32[]{:S(2)}, u32[]{:S(2)}) collective-permute-start(f32[4,128,128]{2,1,0:T(8,128)S(1)} %get-tuple-element.13), channel_id=1, source_target_pairs={{4,0},{8,4},{12,8},{16,12},{20,16},{24,20},{28,24},{5,1},{9,5},{13... | collective-permute-start | bytes 786440 | tf_op jit(solution)/shard_map/ppermute | solution.py:22
  379.6 1.1 fusion.80
  380.7 3.3 collective-permute-start.22
  384.0 1.3 collective-permute-start.23
  385.3 1.2 collective-permute-done.22
  386.5 4.4 %collective-permute-done.23 = f32[64,4,128]{2,1,0:T(4,128)S(1)} collective-permute-done((f32[64,4,128]{2,1,0:T(4,128)S(1)}, f32[64,4,128]{2,1,0:T(4,128)S(1)}, u32[]{:S(2)}, u32[]{:S(2)}) %collective-permute-start.23) | collective-permute-done | bytes 131104 | tf_op jit(solution)/shard_map/ppermute | solution.py:22
  390.9 5.5 %fusion.62 = f32[64,128,128]{2,1,0:T(8,128)} fusion(f32[64,128,128]{2,1,0:T(8,128)S(1)} %fusion.77, f32[72,136,128]{2,1,0:T(8,128)} %fusion.54, f32[64,4,128]{2,1,0:T(4,128)S(1)} %collective-permute-done.23, f32[64,4,128]{2,1,0:T(4,128)S(1)} %collective-permute-done.22, f32[4,128,128]{2,1,0:T(8,128)S(1)} %collective-permute-done.21, ...), kind=kLoop, calls=%fused_computation.94 | loop fusion | flops 6291456 | bytes 13402112 | tf_op jit(solution)/shard_map/add | solution.py:167
  (83 shorter events, 7.0 us)
Async XLA Ops:
  0.0 17.5 %copy-start.14 = (s32[2,128]{1,0:T(2,128)S(1)}, s32[2,128]{1,0:T(2,128)}, u32[]{:S(2)}) copy-start(s32[2,128]{1,0:T(2,128)} %param.8) | copy-start | bytes 3076
  0.0 17.5 %copy-start.15 = (s32[64,2]{0,1:T(2,128)S(1)}, s32[64,2]{0,1:T(2,128)}, u32[]{:S(2)}) copy-start(s32[64,2]{0,1:T(2,128)} %param.9) | copy-start | bytes 1540
  2.5 22.7 %collective-permute-start.4 = (f32[2,5,128,128]{3,0,2,1:T(2,128)S(1)}, f32[2,5,128,128]{3,0,2,1:T(2,128)S(1)}, u32[]{:S(2)}, u32[]{:S(2)}) collective-permute-start(f32[2,5,128,128]{3,0,2,1:T(2,128)S(1)} %get-tuple-element.10), channel_id=1, source_target_pairs={{0,4},{4,8},{8,12},{12,16},{16,20},{20,24},{24,28},{1,5},{5,9},{9,... | collective-permute-start | bytes 1966088 | tf_op jit(solution)/shard_map/ppermute | solution.py:19
  4.4 20.8 %collective-permute-start.5 = (f32[2,5,128,128]{3,0,2,1:T(2,128)S(1)}, f32[2,5,128,128]{3,0,2,1:T(2,128)S(1)}, u32[]{:S(2)}, u32[]{:S(2)}) collective-permute-start(f32[2,5,128,128]{3,0,2,1:T(2,128)S(1)} %get-tuple-element.11), channel_id=1, source_target_pairs={{4,0},{8,4},{12,8},{16,12},{20,16},{24,20},{28,24},{5,1},{9,5},{13... | collective-permute-start | bytes 1966088 | tf_op jit(solution)/shard_map/ppermute | solution.py:22
  10.7 14.4 %collective-permute-start = (f32[4,128,128]{2,1,0:T(8,128)S(1)}, f32[4,128,128]{2,1,0:T(8,128)S(1)}, u32[]{:S(2)}, u32[]{:S(2)}) collective-permute-start(f32[4,128,128]{2,1,0:T(8,128)S(1)} %get-tuple-element.41), channel_id=1, source_target_pairs={{0,4},{4,8},{8,12},{12,16},{16,20},{20,24},{24,28},{1,5},{5,9},{9,... | collective-permute-start | bytes 786440 | tf_op jit(solution)/shard_map/ppermute | solution.py:19
  12.6 21.7 %collective-permute-start.1 = (f32[4,128,128]{2,1,0:T(8,128)}, f32[4,128,128]{2,1,0:T(8,128)}, u32[]{:S(2)}, u32[]{:S(2)}) collective-permute-start(f32[4,128,128]{2,1,0:T(8,128)} %get-tuple-element.40), channel_id=1, source_target_pairs={{4,0},{8,4},{12,8},{16,12},{20,16},{24,20},{28,24},{5,1},{9,5},{13... | collective-permute-start | bytes 786440 | tf_op jit(solution)/shard_map/ppermute | solution.py:22
  25.1 8.7 %copy-start.5 = (f32[64,128,128]{2,1,0:T(8,128)S(1)}, f32[64,128,128]{2,1,0:T(8,128)}, u32[]{:S(2)}) copy-start(f32[64,128,128]{2,1,0:T(8,128)} %param.7) | copy-start | bytes 12582916
  25.1 0.9 copy-start.6
  26.0 0.8 copy-start.8
  28.7 14.0 %copy-start.1 = (f32[64,128,128]{2,1,0:T(8,128)S(1)}, f32[64,128,128]{2,1,0:T(8,128)}, u32[]{:S(2)}) copy-start(f32[64,128,128]{2,1,0:T(8,128)} %param.6) | copy-start | bytes 12582916
  28.7 14.0 %copy-start.2 = (f32[64,128,128]{2,1,0:T(8,128)S(1)}, f32[64,128,128]{2,1,0:T(8,128)}, u32[]{:S(2)}) copy-start(f32[64,128,128]{2,1,0:T(8,128)} %param.5) | copy-start | bytes 12582916
  28.7 14.0 %copy-start.7 = (f32[2,5,128,128]{3,0,2,1:T(2,128)S(1)}, f32[2,5,128,128]{3,0,2,1:T(2,128)}, u32[]{:S(2)}) copy-start(f32[2,5,128,128]{3,0,2,1:T(2,128)} %copy-done.6) | copy-start | bytes 1966084
  28.7 13.3 %collective-permute-start.6 = (f32[2,74,5,128]{3,0,2,1:T(2,128)S(1)}, f32[2,74,5,128]{3,0,2,1:T(2,128)S(1)}, u32[]{:S(2)}, u32[]{:S(2)}) collective-permute-start(f32[2,74,5,128]{3,0,2,1:T(2,128)S(1)} %get-tuple-element.8), channel_id=1, source_target_pairs={{0,1},{1,2},{2,3},{4,5},{5,6},{6,7},{8,9},{9,10},{10,11},{12,13},{... | collective-permute-start | bytes 1136648 | tf_op jit(solution)/shard_map/ppermute | solution.py:19
  32.5 10.2 %collective-permute-start.7 = (f32[2,74,5,128]{3,0,2,1:T(2,128)S(1)}, f32[2,74,5,128]{3,0,2,1:T(2,128)S(1)}, u32[]{:S(2)}, u32[]{:S(2)}) collective-permute-start(f32[2,74,5,128]{3,0,2,1:T(2,128)S(1)} %get-tuple-element.9), channel_id=1, source_target_pairs={{1,0},{2,1},{3,2},{5,4},{6,5},{7,6},{9,8},{10,9},{11,10},{13,12},{... | collective-permute-start | bytes 1136648 | tf_op jit(solution)/shard_map/ppermute | solution.py:22
  35.3 33.3 %copy-start.4 = (f32[72,128,128]{2,1,0:T(8,128)}, f32[72,128,128]{2,1,0:T(8,128)S(1)}, u32[]{:S(2)}) copy-start(f32[72,128,128]{2,1,0:T(8,128)S(1)} %constant_dynamic-update-slice_fusion) | copy-start | bytes 14155780
  35.3 90.4 %collective-permute-start.2 = (f32[72,4,128]{2,1,0:T(4,128)S(1)}, f32[72,4,128]{2,1,0:T(4,128)}, u32[]{:S(2)}, u32[]{:S(2)}) collective-permute-start(f32[72,4,128]{2,1,0:T(4,128)S(1)} %get-tuple-element.30), channel_id=1, source_target_pairs={{0,1},{1,2},{2,3},{4,5},{5,6},{6,7},{8,9},{9,10},{10,11},{12,13},{... | collective-permute-start | bytes 442376 | tf_op jit(solution)/shard_map/ppermute | solution.py:19
  40.5 85.2 %collective-permute-start.3 = (f32[72,4,128]{2,1,0:T(4,128)S(1)}, f32[72,4,128]{2,1,0:T(4,128)}, u32[]{:S(2)}, u32[]{:S(2)}) collective-permute-start(f32[72,4,128]{2,1,0:T(4,128)S(1)} %get-tuple-element.31), channel_id=1, source_target_pairs={{1,0},{2,1},{3,2},{5,4},{6,5},{7,6},{9,8},{10,9},{11,10},{13,12},{... | collective-permute-start | bytes 442376 | tf_op jit(solution)/shard_map/ppermute | solution.py:22
  76.0 2.2 copy-start.3
  76.0 2.3 copy-start.9
  217.0 18.5 %collective-permute-start.8 = (f32[4,128,128]{2,1,0:T(8,128)S(1)}, f32[4,128,128]{2,1,0:T(8,128)S(1)}, u32[]{:S(2)}, u32[]{:S(2)}) collective-permute-start(f32[4,128,128]{2,1,0:T(8,128)S(1)} %get-tuple-element.20), channel_id=1, source_target_pairs={{0,4},{4,8},{8,12},{12,16},{16,20},{20,24},{24,28},{1,5},{5,9},{9,... | collective-permute-start | bytes 786440 | tf_op jit(solution)/shard_map/ppermute | solution.py:19
  219.0 16.6 %collective-permute-start.9 = (f32[4,128,128]{2,1,0:T(8,128)S(1)}, f32[4,128,128]{2,1,0:T(8,128)S(1)}, u32[]{:S(2)}, u32[]{:S(2)}) collective-permute-start(f32[4,128,128]{2,1,0:T(8,128)S(1)} %get-tuple-element.21), channel_id=1, source_target_pairs={{4,0},{8,4},{12,8},{16,12},{20,16},{24,20},{28,24},{5,1},{9,5},{13... | collective-permute-start | bytes 786440 | tf_op jit(solution)/shard_map/ppermute | solution.py:22
  224.6 6.6 %collective-permute-start.10 = (f32[64,4,128]{2,1,0:T(4,128)S(1)}, f32[64,4,128]{2,1,0:T(4,128)S(1)}, u32[]{:S(2)}, u32[]{:S(2)}) collective-permute-start(f32[64,4,128]{2,1,0:T(4,128)S(1)} %get-tuple-element.22), channel_id=1, source_target_pairs={{0,1},{1,2},{2,3},{4,5},{5,6},{6,7},{8,9},{9,10},{10,11},{12,13},{... | collective-permute-start | bytes 393224 | tf_op jit(solution)/shard_map/ppermute | solution.py:19
  228.7 6.9 %collective-permute-start.11 = (f32[64,4,128]{2,1,0:T(4,128)S(1)}, f32[64,4,128]{2,1,0:T(4,128)S(1)}, u32[]{:S(2)}, u32[]{:S(2)}) collective-permute-start(f32[64,4,128]{2,1,0:T(4,128)S(1)} %get-tuple-element.23), channel_id=1, source_target_pairs={{1,0},{2,1},{3,2},{5,4},{6,5},{7,6},{9,8},{10,9},{11,10},{13,12},{... | collective-permute-start | bytes 393224 | tf_op jit(solution)/shard_map/ppermute | solution.py:22
  239.3 6.5 %collective-permute-start.12 = (f32[1,128,128]{2,1,0:T(8,128)S(1)}, f32[1,128,128]{2,1,0:T(8,128)S(1)}, u32[]{:S(2)}, u32[]{:S(2)}) collective-permute-start(f32[1,128,128]{2,1,0:T(8,128)S(1)} %get-tuple-element.38), channel_id=1, source_target_pairs={{0,4},{4,8},{8,12},{12,16},{16,20},{20,24},{24,28},{1,5},{5,9},{9,... | collective-permute-start | bytes 196616 | tf_op jit(solution)/shard_map/ppermute | solution.py:19
  241.2 6.4 %collective-permute-start.13 = (f32[1,128,128]{2,1,0:T(8,128)S(1)}, f32[1,128,128]{2,1,0:T(8,128)S(1)}, u32[]{:S(2)}, u32[]{:S(2)}) collective-permute-start(f32[1,128,128]{2,1,0:T(8,128)S(1)} %get-tuple-element.39), channel_id=1, source_target_pairs={{4,0},{8,4},{12,8},{16,12},{20,16},{24,20},{28,24},{5,1},{9,5},{13... | collective-permute-start | bytes 196616 | tf_op jit(solution)/shard_map/ppermute | solution.py:22
  247.7 10.0 %collective-permute-start.14 = (f32[66,1,128]{2,1,0:T(1,128)S(1)}, f32[66,1,128]{2,1,0:T(1,128)S(1)}, u32[]{:S(2)}, u32[]{:S(2)}) collective-permute-start(f32[66,1,128]{2,1,0:T(1,128)S(1)} %get-tuple-element.32), channel_id=1, source_target_pairs={{0,1},{1,2},{2,3},{4,5},{5,6},{6,7},{8,9},{9,10},{10,11},{12,13},{... | collective-permute-start | bytes 101384 | tf_op jit(solution)/shard_map/ppermute | solution.py:19
  251.2 6.5 %slice-start = ((s8[5013504]{0:T(1024)(128)(4,1)}), s8[4194304]{0:T(1024)(128)(4,1)S(1)}, s32[]{:S(2)}) async-start(s8[5013504]{0:T(1024)(128)(4,1)} %bitcast.15), calls=%async_computation | async-start | bytes 8388608
  251.2 6.5 %slice-start.1 = ((s8[5013504]{0:T(1024)(128)(4,1)}), s8[819200]{0:T(1024)(128)(4,1)S(1)}, s32[]{:S(2)}) async-start(s8[5013504]{0:T(1024)(128)(4,1)} %bitcast.15), calls=%async_computation.1 | async-start | bytes 1638400
  251.2 6.5 %collective-permute-start.15 = (f32[66,1,128]{2,1,0:T(1,128)S(1)}, f32[66,1,128]{2,1,0:T(1,128)S(1)}, u32[]{:S(2)}, u32[]{:S(2)}) collective-permute-start(f32[66,1,128]{2,1,0:T(1,128)S(1)} %get-tuple-element.33), channel_id=1, source_target_pairs={{1,0},{2,1},{3,2},{5,4},{6,5},{7,6},{9,8},{10,9},{11,10},{13,12},{... | collective-permute-start | bytes 101384 | tf_op jit(solution)/shard_map/ppermute | solution.py:22
  272.4 25.1 %copy-start = (f32[64,128,128]{2,1,0:T(8,128)S(1)}, f32[64,128,128]{2,1,0:T(8,128)}, u32[]{:S(2)}) copy-start(f32[64,128,128]{2,1,0:T(8,128)} %fusion.68) | copy-start | bytes 12582916
  273.6 9.1 %collective-permute-start.16 = (f32[4,128,128]{2,1,0:T(8,128)S(1)}, f32[4,128,128]{2,1,0:T(8,128)S(1)}, u32[]{:S(2)}, u32[]{:S(2)}) collective-permute-start(f32[4,128,128]{2,1,0:T(8,128)S(1)} %get-tuple-element.34), channel_id=1, source_target_pairs={{0,4},{4,8},{8,12},{12,16},{16,20},{20,24},{24,28},{1,5},{5,9},{9,... | collective-permute-start | bytes 786440 | tf_op jit(solution)/shard_map/ppermute | solution.py:19
  275.7 8.4 %collective-permute-start.17 = (f32[4,128,128]{2,1,0:T(8,128)S(1)}, f32[4,128,128]{2,1,0:T(8,128)S(1)}, u32[]{:S(2)}, u32[]{:S(2)}) collective-permute-start(f32[4,128,128]{2,1,0:T(8,128)S(1)} %get-tuple-element.35), channel_id=1, source_target_pairs={{4,0},{8,4},{12,8},{16,12},{20,16},{24,20},{28,24},{5,1},{9,5},{13... | collective-permute-start | bytes 786440 | tf_op jit(solution)/shard_map/ppermute | solution.py:22
  282.7 14.2 %copy-start.10 = (f32[4,128,128]{2,1,0:T(8,128)}, f32[4,128,128]{2,1,0:T(8,128)S(1)}, u32[]{:S(2)}) copy-start(f32[4,128,128]{2,1,0:T(8,128)S(1)} %collective-permute-done.16) | copy-start | bytes 786436
  284.1 12.8 %copy-start.11 = (f32[4,128,128]{2,1,0:T(8,128)}, f32[4,128,128]{2,1,0:T(8,128)S(1)}, u32[]{:S(2)}) copy-start(f32[4,128,128]{2,1,0:T(8,128)S(1)} %collective-permute-done.17) | copy-start | bytes 786436
  285.3 7.2 %collective-permute-start.18 = (f32[72,4,128]{2,1,0:T(4,128)S(1)}, f32[72,4,128]{2,1,0:T(4,128)S(1)}, u32[]{:S(2)}, u32[]{:S(2)}) collective-permute-start(f32[72,4,128]{2,1,0:T(4,128)S(1)} %get-tuple-element.28), channel_id=1, source_target_pairs={{0,1},{1,2},{2,3},{4,5},{5,6},{6,7},{8,9},{9,10},{10,11},{12,13},{... | collective-permute-start | bytes 442376 | tf_op jit(solution)/shard_map/ppermute | solution.py:19
  289.8 7.0 %collective-permute-start.19 = (f32[72,4,128]{2,1,0:T(4,128)S(1)}, f32[72,4,128]{2,1,0:T(4,128)S(1)}, u32[]{:S(2)}, u32[]{:S(2)}) collective-permute-start(f32[72,4,128]{2,1,0:T(4,128)S(1)} %get-tuple-element.29), channel_id=1, source_target_pairs={{1,0},{2,1},{3,2},{5,4},{6,5},{7,6},{9,8},{10,9},{11,10},{13,12},{... | collective-permute-start | bytes 442376 | tf_op jit(solution)/shard_map/ppermute | solution.py:22
  292.5 4.4 %copy-start.12 = (f32[72,4,128]{2,1,0:T(4,128)}, f32[72,4,128]{2,1,0:T(4,128)S(1)}, u32[]{:S(2)}) copy-start(f32[72,4,128]{2,1,0:T(4,128)S(1)} %collective-permute-done.18) | copy-start | bytes 442372
  296.9 0.7 copy-start.13
  373.1 17.7 %collective-permute-start.20 = (f32[4,128,128]{2,1,0:T(8,128)S(1)}, f32[4,128,128]{2,1,0:T(8,128)S(1)}, u32[]{:S(2)}, u32[]{:S(2)}) collective-permute-start(f32[4,128,128]{2,1,0:T(8,128)S(1)} %get-tuple-element.12), channel_id=1, source_target_pairs={{0,4},{4,8},{8,12},{12,16},{16,20},{20,24},{24,28},{1,5},{5,9},{9,... | collective-permute-start | bytes 786440 | tf_op jit(solution)/shard_map/ppermute | solution.py:19
  375.0 15.8 %collective-permute-start.21 = (f32[4,128,128]{2,1,0:T(8,128)S(1)}, f32[4,128,128]{2,1,0:T(8,128)S(1)}, u32[]{:S(2)}, u32[]{:S(2)}) collective-permute-start(f32[4,128,128]{2,1,0:T(8,128)S(1)} %get-tuple-element.13), channel_id=1, source_target_pairs={{4,0},{8,4},{12,8},{16,12},{20,16},{24,20},{28,24},{5,1},{9,5},{13... | collective-permute-start | bytes 786440 | tf_op jit(solution)/shard_map/ppermute | solution.py:22
  380.7 5.8 %collective-permute-start.22 = (f32[64,4,128]{2,1,0:T(4,128)S(1)}, f32[64,4,128]{2,1,0:T(4,128)S(1)}, u32[]{:S(2)}, u32[]{:S(2)}) collective-permute-start(f32[64,4,128]{2,1,0:T(4,128)S(1)} %get-tuple-element.14), channel_id=1, source_target_pairs={{0,1},{1,2},{2,3},{4,5},{5,6},{6,7},{8,9},{9,10},{10,11},{12,13},{... | collective-permute-start | bytes 393224 | tf_op jit(solution)/shard_map/ppermute | solution.py:19
  384.0 6.9 %collective-permute-start.23 = (f32[64,4,128]{2,1,0:T(4,128)S(1)}, f32[64,4,128]{2,1,0:T(4,128)S(1)}, u32[]{:S(2)}, u32[]{:S(2)}) collective-permute-start(f32[64,4,128]{2,1,0:T(4,128)S(1)} %get-tuple-element.15), channel_id=1, source_target_pairs={{1,0},{2,1},{3,2},{5,4},{6,5},{7,6},{9,8},{10,9},{11,10},{13,12},{... | collective-permute-start | bytes 393224 | tf_op jit(solution)/shard_map/ppermute | solution.py:22
where the time goes:
time: 401 us; the launch traced here: 397 us
  other arithmetic  235 us (59%)
  starting transfers between devices  71.5 us (18%)
  local copies, waits for them, and re-layouts  59.7 us (15%)
  waiting for transfers between devices  30.1 us (8%)
    select_n x6, other arithmetic, local_solve(): jnp.where(member_cells, (resid_ext + neighbour_sum(padded, coeffs)) / dia...  126 us
    slice x1, other arithmetic, shards(): widened[1, 1:-1, 1:-1]  43.3 us
    slice x5, local copies, waits for them, and re-layouts, neighbour_sum(): below = jnp.concatenate([bottom, centre[:, :, :-1]], axis=2)  41.3 us
    ppermute x12, starting transfers between devices, padded_2(): lax.ppermute(lax.slice_in_dim(block, block.shape[dim] - width, None, axis...  36 us
    ppermute x12, starting transfers between devices, padded_2(): lax.ppermute(lax.slice_in_dim(block, 0, width, axis=dim), axis, backward)  35.4 us
    concatenate x1, other arithmetic, padded_2(): block = jnp.concatenate([low, block, high], axis=dim)  25.8 us
    ppermute x12, waiting for transfers between devices, padded_2(): lax.ppermute(lax.slice_in_dim(block, 0, width, axis=dim), axis, backward)  17.1 us
    sub x1, other arithmetic, shards(): residual = rhs - operate(nearby, own_coeffs)  14.6 us
  transfers between devices with their start and end apart: 24, of which 11 were waited for; matrix products, arithmetic and copies ran while one was open for 24% of the time, Pallas kernels for 0%

commit v1 on v0

v1 whole, which is shorter than its diff:
```python
import functools

import jax
import jax.numpy as jnp
from jax import lax
from jax.experimental import pallas as pl
from jax.experimental.pallas import tpu as pltpu
from jax.sharding import PartitionSpec as P

OVL = 4
VERTICAL = 0.1
MESH = pl.DeviceIdType.MESH

PADX = 5
PADY = 8
DIRS = ((-1, 0), (1, 0), (0, -1), (0, 1), (-1, -1), (-1, 1), (1, -1), (1, 1))


def recip(value):
    guess = pl.reciprocal(value, approx=True)
    return guess * (2.0 - value * guess)


def harmonic(first, second):
    return 2.0 * first * second * recip(first + second)


def kernel(n_sub, n_col, bx, by, perm, accum, rhs, dx_ref, dy_ref, out,
           pm, w, r, b, c, fx, fy, fz, pr, sx, sy, ssem, rsem, lsem):
    nz = 128
    s = lax.axis_index("sub")
    k = lax.axis_index("col")
    ex, ey = bx + 2 * PADX, by + 2 * PADY
    nbx, nby = (bx + 8) // 8, (by + 8) // 8
    x_end, y_end = PADX + bx, PADY + by

    def exists(d):
        ok = None
        for coord, step, count in ((s, d[0], n_sub), (k, d[1], n_col)):
            if step == -1:
                test = coord > 0
            elif step == 1:
                test = coord < count - 1
            else:
                continue
            ok = test if ok is None else ok & test
        return ok

    def device(d):
        return (s + d[0], k + d[1])

    own_x, own_y = pl.ds(PADX, bx), pl.ds(PADY, by)
    local = [
        pltpu.make_async_copy(src, dst.at[own_x, own_y, :], lsem.at[i])
        for i, (src, dst) in enumerate(((perm, pm), (accum, w), (rhs, r)))
    ]
    for copy in local:
        copy.start()

    def fill(ref, value):
        ref[0:PADX, :, :] = jnp.full((PADX, ey, nz), value, jnp.float32)
        ref[x_end:ex, :, :] = jnp.full((PADX, ey, nz), value, jnp.float32)
        ref[PADX:x_end, 0:PADY, :] = jnp.full((bx, PADY, nz), value, jnp.float32)
        ref[PADX:x_end, y_end:ey, :] = jnp.full((bx, PADY, nz), value, jnp.float32)

    fill(pm, 1.0)
    fill(w, 1.0)
    fill(r, 0.0)
    fill(b, 0.0)
    fill(c, 0.0)
    fill(pr, 0.0)
    sx[...] = jnp.zeros(sx.shape, jnp.float32)
    sy[...] = jnp.zeros(sy.shape, jnp.float32)

    barrier = pltpu.get_barrier_semaphore()
    arrivals = jnp.int32(0)
    for d in DIRS:
        @pl.when(exists(d))
        def _(d=d):
            pl.semaphore_signal(barrier, inc=1, device_id=device(d), device_id_type=MESH)
        arrivals = arrivals + jnp.where(exists(d), 1, 0).astype(jnp.int32)
    pl.semaphore_wait(barrier, arrivals)

    counter = [0]

    def remote(src, dst, d):
        i = counter[0]
        counter[0] += 1
        return d, pltpu.make_async_remote_copy(
            src_ref=src, dst_ref=dst, send_sem=ssem.at[i], recv_sem=rsem.at[i],
            device_id=device(d), device_id_type=MESH)

    def start(copies):
        for d, copy in copies:
            pl.when(exists(d))(copy.start)

    def wait_recv(copies):
        for d, copy in copies:
            pl.when(exists((-d[0], -d[1])))(copy.wait_recv)

    def wait_send(copies):
        for d, copy in copies:
            pl.when(exists(d))(copy.wait_send)

    def halo(src, ox, oy, dst, d, width):
        def span(step, offset, extent, pad, thick):
            if step == 0:
                return pl.ds(offset, extent), pl.ds(pad, extent)
            if step == 1:
                return pl.ds(offset + extent - thick, thick), pl.ds(pad - thick, thick)
            return pl.ds(offset, thick), pl.ds(pad + extent, thick)

        sxs, dxs = span(d[0], ox, bx, PADX, width)
        sys_, dys = span(d[1], oy, by, PADY, YW(width))
        return remote(src.at[sxs, sys_, :], dst.at[dxs, dys, :], d)

    def YW(width):
        return 8

    halos = [halo(perm, 0, 0, pm, d, 5) for d in DIRS]
    halos += [halo(accum, 0, 0, w, d, 4) for d in DIRS[:4]]
    halos += [halo(rhs, 0, 0, r, d, 4) for d in DIRS[:4]]
    start(halos)

    def at(ref, x0, y0, rows=8, columns=8):
        return ref[pl.ds(x0, rows), pl.ds(y0, columns), :]

    def stencil(ref, x0, y0):
        wide = at(ref, x0 - 1, y0, 10)
        centre = wide[1:9]
        face = at(fx, x0 - 1, y0, 9)
        total = face[0:8] * wide[0:8] + face[1:9] * wide[2:10]
        total = total + at(fy, x0, y0) * at(ref, x0, y0 - 1)
        total = total + at(fy, x0, y0 + 1) * at(ref, x0, y0 + 1)
        up = at(fz, x0, y0)
        total = total + up * pltpu.roll(centre, nz - 1, 2)
        total = total + pltpu.roll(up * centre, 1, 2)
        return total, centre

    def coefficients(x0, y0, frame):
        wide = at(pm, x0 - 1, y0, 10)
        centre = wide[1:9]
        across_x = harmonic(wide[0:9], wide[1:10])
        across_y0 = harmonic(at(pm, x0, y0 - 1), centre)
        across_y1 = harmonic(centre, at(pm, x0, y0 + 1))
        lane = lax.broadcasted_iota(jnp.int32, (8, 8, nz), 2)
        up = VERTICAL * harmonic(centre, pltpu.roll(centre, nz - 1, 2))
        up = jnp.where(lane < nz - 1, up, 0.0)
        if frame:
            row = x0 - 1 + lax.broadcasted_iota(jnp.int32, (9, 8, nz), 0)
            shut = (row == jnp.where(s == 0, PADX - 1, -1)) | (
                row == jnp.where(s == n_sub - 1, x_end - 1, -1))
            across_x = jnp.where(shut, 0.0, across_x)
            column = y0 + lax.broadcasted_iota(jnp.int32, (8, 8, nz), 1)
            first = jnp.where(k == 0, PADY, -1)
            last = jnp.where(k == n_col - 1, y_end, -1)
            across_y0 = jnp.where((column == first) | (column == last), 0.0, across_y0)
            across_y1 = jnp.where((column + 1 == first) | (column + 1 == last), 0.0, across_y1)
        diagonal = (at(w, x0, y0) + across_x[0:8] + across_x[1:9] + across_y0 + across_y1
                    + up + pltpu.roll(up, 1, 2))
        inverse = recip(diagonal)
        if frame:
            row = row[0:8] + 1
            low_x, high_x = dx_ref[0, pl.ds(y0, 8), :], dx_ref[1, pl.ds(y0, 8), :]
            low_y, high_y = dy_ref[0, pl.ds(x0, 8), :, :], dy_ref[1, pl.ds(x0, 8), :, :]
            member = (row >= PADX) & (row < x_end) & (column >= PADY) & (column < y_end)
            member = member | ((row < PADX) & (PADX - 1 - row < low_x[None]))
            member = member | ((row >= x_end) & (row - x_end < high_x[None]))
            member = member | ((column < PADY) & (PADY - 1 - column < low_y))
            member = member | ((column >= y_end) & (column - y_end < high_y))
            inverse = jnp.where(member, inverse, 0.0)
        fx[pl.ds(x0 - 1, 9), pl.ds(y0, 8), :] = across_x
        fy[pl.ds(x0, 8), pl.ds(y0, 8), :] = across_y0
        fy[pl.ds(x0, 8), pl.ds(y0 + 1, 8), :] = across_y1
        fz[pl.ds(x0, 8), pl.ds(y0, 8), :] = up
        w[pl.ds(x0, 8), pl.ds(y0, 8), :] = inverse
        b[pl.ds(x0, 8), pl.ds(y0, 8), :] = inverse * at(r, x0, y0)

    def second_sweep(x0, y0):
        total, _ = stencil(b, x0, y0)
        c[pl.ds(x0, 8), pl.ds(y0, 8), :] = at(b, x0, y0) + at(w, x0, y0) * total

    def third_sweep(x0, y0):
        total, _ = stencil(c, x0, y0)
        return at(b, x0, y0) + at(w, x0, y0) * total

    def third_frame(x0, y0):
        b[pl.ds(x0, 8), pl.ds(y0, 8), :] = third_sweep(x0, y0)

    def third_first(x0, y0):
        pr[pl.ds(x0, 8), pl.ds(y0, 8), :] = third_sweep(x0, y0)

    def third_last(x0, y0):
        pr[pl.ds(x0, 8), pl.ds(y0, 8), :] = at(pr, x0, y0) + third_sweep(x0, y0)

    def restart(x0, y0):
        total, centre = stencil(pr, x0, y0)
        weight = at(w, x0, y0)
        b[pl.ds(x0, 8), pl.ds(y0, 8), :] = jnp.where(
            weight > 0.0, weight * (at(r, x0, y0) + total) - centre, 0.0)

    def interior(body):
        def outer(j, carry):
            def inner(i, carry):
                body(1 + 8 * i, 4 + 8 * j)
                return carry
            return lax.fori_loop(1, nbx - 1, inner, carry)
        lax.fori_loop(1, nby - 1, outer, 0)

    def frame(body):
        def along_y(j, carry):
            body(1, 4 + 8 * j)
            body(1 + 8 * (nbx - 1), 4 + 8 * j)
            return carry
        lax.fori_loop(0, nby, along_y, 0)

        def along_x(i, carry):
            body(1 + 8 * i, 4)
            body(1 + 8 * i, 4 + 8 * (nby - 1))
            return carry
        lax.fori_loop(1, nbx - 1, along_x, 0)

    def gather(turn, x0, y0, side_x, side_y):
        own = at(b, x0, y0, 4)
        before = at(pr, x0, y0, 4)
        row = x0 + lax.broadcasted_iota(jnp.int32, (4, 8, nz), 0)
        column = y0 + lax.broadcasted_iota(jnp.int32, (4, 8, nz), 1)
        total = own
        if side_x is not None:
            total = total + sx[turn, side_x, :, pl.ds(y0 - PADY, 8), :]
        if side_y is not None:
            total = total + sy[turn, side_y, pl.ds(x0 - PADX, 4), :, :]
        cover = 1.0 + (row - PADX < dx_ref[0, pl.ds(y0, 8), :][None]).astype(jnp.float32)
        cover = cover + (x_end - 1 - row < dx_ref[1, pl.ds(y0, 8), :][None]).astype(jnp.float32)
        cover = cover + (column - PADY < dy_ref[0, pl.ds(x0, 4), :, :]).astype(jnp.float32)
        cover = cover + (y_end - 1 - column < dy_ref[1, pl.ds(x0, 4), :, :]).astype(jnp.float32)
        total = total / cover
        if turn == 1:
            total = before + total
        if side_x is None:
            edge = (column < PADY + 4) if side_y == 0 else (column >= y_end - 4)
            total = jnp.where(edge, total, before)
        pr[pl.ds(x0, 4), pl.ds(y0, 8), :] = total

    def gather_all(turn):
        top = x_end - 4
        for side_y, y0 in ((0, PADY), (1, y_end - 8)):
            gather(turn, PADX, y0, 0, side_y)
            gather(turn, top, y0, 1, side_y)

            def along_x(i, carry, y0=y0, side_y=side_y):
                gather(turn, PADX + 4 * i, y0, None, side_y)
                return carry
            lax.fori_loop(1, bx // 4 - 1, along_x, 0)

        def along_y(j, carry):
            gather(turn, PADX, PADY + 8 * j, 0, None)
            gather(turn, top, PADY + 8 * j, 1, None)
            return carry
        lax.fori_loop(1, by // 8 - 1, along_y, 0)

    def returns(turn):
        return [
            remote(b.at[pl.ds(PADX - 4, 4), own_y, :], sx.at[turn, 1], (-1, 0)),
            remote(b.at[pl.ds(x_end, 4), own_y, :], sx.at[turn, 0], (1, 0)),
            remote(b.at[own_x, pl.ds(0, 8), :], sy.at[turn, 1], (0, -1)),
            remote(b.at[own_x, pl.ds(y_end, 8), :], sy.at[turn, 0], (0, 1)),
        ]

    for copy in local:
        copy.wait()
    interior(functools.partial(coefficients, frame=False))
    wait_recv(halos)
    frame(functools.partial(coefficients, frame=True))
    interior(second_sweep)
    frame(second_sweep)
    frame(third_frame)
    back = returns(0)
    start(back)
    interior(third_first)
    wait_recv(back)
    gather_all(0)
    spread = [halo(pr, PADX, PADY, pr, d, 5) for d in DIRS]
    start(spread)
    wait_send(back)
    interior(restart)
    wait_recv(spread)
    frame(restart)
    interior(second_sweep)
    frame(second_sweep)
    frame(third_frame)
    back = returns(1)
    start(back)
    wait_send(spread)
    interior(third_last)
    wait_recv(back)
    gather_all(1)
    final = pltpu.make_async_copy(pr.at[own_x, own_y, :], out, lsem.at[0])
    final.start()
    wait_send(halos)
    wait_send(back)
    final.wait()


def shards(n_sub, n_col, perm, accum, rhs, depth_x, depth_y):
    bx, by, nz = perm.shape
    ex, ey = bx + 2 * PADX, by + 2 * PADY
    dx = jnp.broadcast_to(jnp.pad(depth_x, ((0, 0), (PADY, PADY)))[:, :, None], (2, ey, nz))
    dy = jnp.broadcast_to(
        jnp.pad(depth_y, ((PADX, PADX), (0, 0))).T[:, :, None, None], (2, ex, 8, nz))
    field = pltpu.VMEM((ex, ey, nz), jnp.float32)
    hbm = pl.BlockSpec(memory_space=pl.ANY)
    vmem = pl.BlockSpec(memory_space=pltpu.VMEM)
    copies = 16 + 4 + 8 + 4
    return pl.pallas_call(
        functools.partial(kernel, n_sub, n_col, bx, by),
        out_shape=jax.ShapeDtypeStruct((bx, by, nz), jnp.float32),
        in_specs=[hbm, hbm, hbm, vmem, vmem],
        out_specs=hbm,
        scratch_shapes=[field] * 9 + [
            pltpu.VMEM((2, 2, 4, by, nz), jnp.float32),
            pltpu.VMEM((2, 2, bx, 8, nz), jnp.float32),
            pltpu.SemaphoreType.DMA((copies,)),
            pltpu.SemaphoreType.DMA((copies,)),
            pltpu.SemaphoreType.DMA((3,)),
        ],
        compiler_params=pltpu.CompilerParams(
            collective_id=0, has_side_effects=True, vmem_limit_bytes=60 * 1024 * 1024),
        cost_estimate=pl.CostEstimate(
            flops=120 * bx * by * nz, bytes_accessed=16 * bx * by * nz, transcendentals=0),
    )(perm, accum, rhs, dx, dy)


def solution(mesh):
    placed = (
        P("sub", "col", None),
        P("sub", "col", None),
        P("sub", "col", None),
        P("sub", "col"),
        P("sub", "col"),
    )
    return jax.shard_map(
        functools.partial(shards, mesh.shape["sub"], mesh.shape["col"]),
        mesh=mesh, in_specs=placed, out_specs=P("sub", "col", None), check_vma=False
    )
```

time: 401 us -> 103 us (0.26)
  other arithmetic: 235 us -> 0 us
  Pallas kernels: 0 us -> 94.1 us
  starting transfers between devices: 71.5 us -> 0 us
  local copies, waits for them, and re-layouts: 59.7 us -> 8 us
  waiting for transfers between devices: 30.1 us -> 0 us
    select_n x9 -> x0, other arithmetic: 131 us -> none  [the longest x6 126 us: local_solve(): jnp.where(member_cells, (resid_ext + neighbour_sum(padded, coeffs)) / dia...]
    pallas_call x0 -> x1, Pallas kernels: none -> 94.1 us  [shards(): pl.pallas_call(functools.partial(kernel, n_sub, n_col, bx, by), out_shape...]
    ppermute x24 -> x0, starting transfers between devices: 71.5 us -> none  [the longest x12 36 us: padded_2(): lax.ppermute(lax.slice_in_dim(block, block.shape[dim] - width, None, axis...]
    slice x18 -> x0, local copies, waits for them, and re-layouts: 55.3 us -> none  [the longest x5 41.3 us: neighbour_sum(): below = jnp.concatenate([bottom, centre[:, :, :-1]], axis=2)]
    slice x5 -> x0, other arithmetic: 48.8 us -> none  [the longest x1 43.3 us: shards(): widened[1, 1:-1, 1:-1]]
    ppermute x24 -> x0, waiting for transfers between devices: 30.1 us -> none  [the longest x12 17.1 us: padded_2(): lax.ppermute(lax.slice_in_dim(block, 0, width, axis=dim), axis, backward)]
    concatenate x1 -> x0, other arithmetic: 25.8 us -> none  [padded_2(): block = jnp.concatenate([low, block, high], axis=dim)]
    sub x5 -> x0, other arithmetic: 14.7 us -> none  [the longest x1 14.6 us: shards(): residual = rhs - operate(nearby, own_coeffs)]
  transfers between devices with their start and end apart: 24 -> 0, of which waited for: 11 -> 0; matrix products, arithmetic and copies ran while one was open for 24% -> 0% of each run, Pallas kernels for 0% -> 0%
where the time goes in v1:
time: 103 us; the launch traced here: 102 us
  Pallas kernels  94.1 us (91%)
  local copies, waits for them, and re-layouts  8 us (8%)
    pallas_call x1, Pallas kernels, shards(): pl.pallas_call(functools.partial(kernel, n_sub, n_col, bx, by), out_shape...  94.1 us
    unnamed x1, local copies, waits for them, and re-layouts  4.7 us

profile of v1, /device:TPU:4, one launch (start us, length us, event | category | flops | bytes accessed | tf_op | source)
XLA Modules:
  0.0 102.1 jit_solution(2431201079241917318)
XLA Ops:
  0.0 0.8 pad_bitcast_fusion
  0.8 0.8 pad.8
  1.5 0.8 broadcast_in_dim.4.dx_ref
  2.3 1.0 %broadcast_in_dim.5.dy_ref = s32[2,74,8,128]{3,2,1,0:T(8,128)} broadcast(s32[2,74]{1,0:T(2,128)S(1)} %pad_bitcast_fusion), dimensions={0,1} | broadcast | bytes 606800 | tf_op jit(solution)/shard_map/broadcast_in_dim | solution.py:309
  3.3 94.1 %shard_map.55 = f32[64,128,128]{2,1,0:T(8,128)} custom-call(f32[64,128,128]{2,1,0:T(8,128)} %perm.1, f32[64,128,128]{2,1,0:T(8,128)} %accum.1, f32[64,128,128]{2,1,0:T(8,128)} %rhs.1, s32[2,144,128]{2,1,0:T(8,128)} %broadcast_in_dim.4.dx_ref, s32[2,74,8,128]{3,2,1,0:T(8,128)} %broadcast_in_dim.5.dy_ref), custom_call_target="tpu_custom_call" | custom-call | flops 125829120 | bytes 16777216 | tf_op jit(solution)/shard_map/pallas_call | solution.py:315
  97.4 4.7 %copy.7 = f32[64,128,128]{2,1,0:T(8,128)} copy(f32[64,128,128]{2,1,0:T(8,128)} %shard_map.55) | data formatting | bytes 8388608

commit v2 on v1

--- a/solution.py
+++ b/solution.py
@@ -25,8 +25,8 @@
     return 2.0 * first * second * recip(first + second)
 
 
-def kernel(n_sub, n_col, bx, by, perm, accum, rhs, dx_ref, dy_ref, out,
-           pm, w, r, b, c, fx, fy, fz, pr, sx, sy, ssem, rsem, lsem):
+def kernel(n_sub, n_col, bx, by, perm, accum, rhs, depth_x, depth_y, out,
+           dx_ref, dy_ref, lane_y, pm, w, r, b, c, fx, fy, fz, pr, sx, sy, ssem, rsem, lsem):
     nz = 128
     s = lax.axis_index("sub")
     k = lax.axis_index("col")
@@ -72,6 +72,17 @@
     sx[...] = jnp.zeros(sx.shape, jnp.float32)
     sy[...] = jnp.zeros(sy.shape, jnp.float32)
 
+    dx_ref[...] = jnp.zeros(dx_ref.shape, jnp.int32)
+    dy_ref[...] = jnp.zeros(dy_ref.shape, jnp.int32)
+    for side in range(2):
+        dx_ref[side, own_y, :] = jnp.broadcast_to(depth_x[side:side + 1, :], (nz, by)).T
+        lane_y[side] = jnp.broadcast_to(depth_y[:, side:side + 1], (bx, nz))
+
+    def spread_depth(i, carry):
+        for side in range(2):
+            dy_ref[side, PADX + i] = jnp.broadcast_to(lane_y[side, pl.ds(i, 1), :], (8, nz))
+        return carry
+
     barrier = pltpu.get_barrier_semaphore()
     arrivals = jnp.int32(0)
     for d in DIRS:
@@ -111,16 +122,14 @@
             return pl.ds(offset, thick), pl.ds(pad + extent, thick)
 
         sxs, dxs = span(d[0], ox, bx, PADX, width)
-        sys_, dys = span(d[1], oy, by, PADY, YW(width))
+        sys_, dys = span(d[1], oy, by, PADY, width)
         return remote(src.at[sxs, sys_, :], dst.at[dxs, dys, :], d)
-
-    def YW(width):
-        return 8
 
     halos = [halo(perm, 0, 0, pm, d, 5) for d in DIRS]
     halos += [halo(accum, 0, 0, w, d, 4) for d in DIRS[:4]]
     halos += [halo(rhs, 0, 0, r, d, 4) for d in DIRS[:4]]
     start(halos)
+    lax.fori_loop(0, bx, spread_depth, 0, unroll=8)
 
     def at(ref, x0, y0, rows=8, columns=8):
         return ref[pl.ds(x0, rows), pl.ds(y0, columns), :]
@@ -199,26 +208,48 @@
         b[pl.ds(x0, 8), pl.ds(y0, 8), :] = jnp.where(
             weight > 0.0, weight * (at(r, x0, y0) + total) - centre, 0.0)
 
+    def loop(low, high, body, unroll):
+        full = (high - low) // unroll
+
+        def several(i, carry):
+            for u in range(unroll):
+                body(low + i * unroll + u)
+            return carry
+        lax.fori_loop(0, full, several, 0)
+        for i in range(low + full * unroll, high):
+            body(i)
+
+    def region(body, x_low, x_high, y_low, y_high):
+        def column(j):
+            for i in range(x_low, x_high):
+                body(1 + 8 * i, 4 + 8 * j)
+        loop(y_low, y_high, column, 1)
+
+    def ring(body, depth, unroll):
+        low_y, high_y = depth, nby - 1 - depth
+        low_x, high_x = depth, nbx - 1 - depth
+
+        def along_y(j):
+            body(1 + 8 * low_x, 4 + 8 * j)
+            body(1 + 8 * high_x, 4 + 8 * j)
+        loop(low_y, high_y + 1, along_y, unroll)
+
+        def along_x(i):
+            body(1 + 8 * i, 4 + 8 * low_y)
+            body(1 + 8 * i, 4 + 8 * high_y)
+        loop(low_x + 1, high_x, along_x, unroll)
+
     def interior(body):
-        def outer(j, carry):
-            def inner(i, carry):
-                body(1 + 8 * i, 4 + 8 * j)
-                return carry
-            return lax.fori_loop(1, nbx - 1, inner, carry)
-        lax.fori_loop(1, nby - 1, outer, 0)
-
-    def frame(body):
-        def along_y(j, carry):
-            body(1, 4 + 8 * j)
-            body(1 + 8 * (nbx - 1), 4 + 8 * j)
-            return carry
-        lax.fori_loop(0, nby, along_y, 0)
-
-        def along_x(i, carry):
-            body(1 + 8 * i, 4)
-            body(1 + 8 * i, 4 + 8 * (nby - 1))
-            return carry
-        lax.fori_loop(1, nbx - 1, along_x, 0)
+        region(body, 1, nbx - 1, 1, nby - 1)
+
+    def inner(body):
+        region(body, 2, nbx - 2, 2, nby - 2)
+
+    def frame(body, unroll=4):
+        ring(body, 0, unroll)
+
+    def border(body):
+        ring(body, 1, 4)
 
     def gather(turn, x0, y0, side_x, side_y):
         own = at(b, x0, y0, 4)
@@ -263,17 +294,18 @@
         return [
             remote(b.at[pl.ds(PADX - 4, 4), own_y, :], sx.at[turn, 1], (-1, 0)),
             remote(b.at[pl.ds(x_end, 4), own_y, :], sx.at[turn, 0], (1, 0)),
-            remote(b.at[own_x, pl.ds(0, 8), :], sy.at[turn, 1], (0, -1)),
-            remote(b.at[own_x, pl.ds(y_end, 8), :], sy.at[turn, 0], (0, 1)),
+            remote(b.at[own_x, pl.ds(4, 4), :], sy.at[turn, 1, :, 4:8, :], (0, -1)),
+            remote(b.at[own_x, pl.ds(y_end, 4), :], sy.at[turn, 0, :, 0:4, :], (0, 1)),
         ]
 
     for copy in local:
         copy.wait()
     interior(functools.partial(coefficients, frame=False))
+    inner(second_sweep)
     wait_recv(halos)
-    frame(functools.partial(coefficients, frame=True))
-    interior(second_sweep)
+    frame(functools.partial(coefficients, frame=True), 1)
     frame(second_sweep)
+    border(second_sweep)
     frame(third_frame)
     back = returns(0)
     start(back)
@@ -282,12 +314,13 @@
     gather_all(0)
     spread = [halo(pr, PADX, PADY, pr, d, 5) for d in DIRS]
     start(spread)
+    interior(restart)
+    inner(second_sweep)
     wait_send(back)
-    interior(restart)
     wait_recv(spread)
     frame(restart)
-    interior(second_sweep)
     frame(second_sweep)
+    border(second_sweep)
     frame(third_frame)
     back = returns(1)
     start(back)
@@ -305,9 +338,6 @@
 def shards(n_sub, n_col, perm, accum, rhs, depth_x, depth_y):
     bx, by, nz = perm.shape
     ex, ey = bx + 2 * PADX, by + 2 * PADY
-    dx = jnp.broadcast_to(jnp.pad(depth_x, ((0, 0), (PADY, PADY)))[:, :, None], (2, ey, nz))
-    dy = jnp.broadcast_to(
-        jnp.pad(depth_y, ((PADX, PADX), (0, 0))).T[:, :, None, None], (2, ex, 8, nz))
     field = pltpu.VMEM((ex, ey, nz), jnp.float32)
     hbm = pl.BlockSpec(memory_space=pl.ANY)
     vmem = pl.BlockSpec(memory_space=pltpu.VMEM)
@@ -317,7 +347,11 @@
         out_shape=jax.ShapeDtypeStruct((bx, by, nz), jnp.float32),
         in_specs=[hbm, hbm, hbm, vmem, vmem],
         out_specs=hbm,
-        scratch_shapes=[field] * 9 + [
+        scratch_shapes=[
+            pltpu.VMEM((2, ey, nz), jnp.int32),
+            pltpu.VMEM((2, ex, 8, nz), jnp.int32),
+            pltpu.VMEM((2, bx, nz), jnp.int32),
+        ] + [field] * 9 + [
             pltpu.VMEM((2, 2, 4, by, nz), jnp.float32),
             pltpu.VMEM((2, 2, bx, 8, nz), jnp.float32),
             pltpu.SemaphoreType.DMA((copies,)),
@@ -328,7 +362,7 @@
             collective_id=0, has_side_effects=True, vmem_limit_bytes=60 * 1024 * 1024),
         cost_estimate=pl.CostEstimate(
             flops=120 * bx * by * nz, bytes_accessed=16 * bx * by * nz, transcendentals=0),
-    )(perm, accum, rhs, dx, dy)
+    )(perm, accum, rhs, depth_x, depth_y)
 
 
 def solution(mesh):

time: 103 us -> 69.3 us (0.67)
  Pallas kernels: 94.1 us -> 62.4 us
  local copies, waits for them, and re-layouts: 8 us -> 6.08 us
    pallas_call x1, Pallas kernels: 94.1 us -> 62.4 us  [shards(): pl.pallas_call(functools.partial(kernel, n_sub, n_col, bx, by), out_shape...]
    broadcast_in_dim x2 -> x0, local copies, waits for them, and re-layouts: 1.8 us -> none  [the longest x1 1.04 us: shards(): jnp.broadcast_to(jnp.pad(depth_y, ((PADX, PADX), (0, 0))).T[:, :, None, N...]
    unnamed x1 -> x2, local copies, waits for them, and re-layouts: 4.7 us -> 6.08 us
where the time goes in v2:
time: 69.3 us; the launch traced here: 68.5 us
  Pallas kernels  62.4 us (90%)
  local copies, waits for them, and re-layouts  6.08 us (9%)
    pallas_call x1, Pallas kernels, shards(): pl.pallas_call(functools.partial(kernel, n_sub, n_col, bx, by), out_shape...  62.4 us
    unnamed x2, local copies, waits for them, and re-layouts  6.08 us

profile of v2, /device:TPU:4, one launch (start us, length us, event | category | flops | bytes accessed | tf_op | source)
XLA Modules:
  0.0 68.5 jit_solution(1988992422252072798)
XLA Ops:
  0.0 1.4 %copy.6.depth_y = s32[64,2]{1,0:T(8,128)} copy(s32[64,2]{0,1:T(2,128)} %param.9) | data formatting | bytes 1024 | tf_op args[4]
  1.4 62.4 %shard_map.55 = f32[64,128,128]{2,1,0:T(8,128)} custom-call(f32[64,128,128]{2,1,0:T(8,128)} %perm.1, f32[64,128,128]{2,1,0:T(8,128)} %accum.1, f32[64,128,128]{2,1,0:T(8,128)} %rhs.1, s32[2,128]{1,0:T(2,128)} %depth_x.1, s32[64,2]{1,0:T(8,128)} %copy.6.depth_y), custom_call_target="tpu_custom_call" | custom-call | flops 125829120 | bytes 16777216 | tf_op jit(solution)/shard_map/pallas_call | solution.py:345
  63.8 4.7 %copy.8 = f32[64,128,128]{2,1,0:T(8,128)} copy(f32[64,128,128]{2,1,0:T(8,128)} %shard_map.55) | data formatting | bytes 8388608

commit v3 on v2

--- a/solution.py
+++ b/solution.py
@@ -17,8 +17,7 @@
 
 
 def recip(value):
-    guess = pl.reciprocal(value, approx=True)
-    return guess * (2.0 - value * guess)
+    return pl.reciprocal(value, approx=True)
 
 
 def harmonic(first, second):
@@ -165,9 +164,8 @@
             last = jnp.where(k == n_col - 1, y_end, -1)
             across_y0 = jnp.where((column == first) | (column == last), 0.0, across_y0)
             across_y1 = jnp.where((column + 1 == first) | (column + 1 == last), 0.0, across_y1)
-        diagonal = (at(w, x0, y0) + across_x[0:8] + across_x[1:9] + across_y0 + across_y1
-                    + up + pltpu.roll(up, 1, 2))
-        inverse = recip(diagonal)
+        faces = (across_x[0:8] + across_x[1:9] + across_y0 + across_y1
+                 + up + pltpu.roll(up, 1, 2))
         if frame:
             row = row[0:8] + 1
             low_x, high_x = dx_ref[0, pl.ds(y0, 8), :], dx_ref[1, pl.ds(y0, 8), :]
@@ -177,11 +175,19 @@
             member = member | ((row >= x_end) & (row - x_end < high_x[None]))
             member = member | ((column < PADY) & (PADY - 1 - column < low_y))
             member = member | ((column >= y_end) & (column - y_end < high_y))
-            inverse = jnp.where(member, inverse, 0.0)
+            c[pl.ds(x0, 8), pl.ds(y0, 8), :] = jnp.where(member, faces, -1.0)
         fx[pl.ds(x0 - 1, 9), pl.ds(y0, 8), :] = across_x
         fy[pl.ds(x0, 8), pl.ds(y0, 8), :] = across_y0
         fy[pl.ds(x0, 8), pl.ds(y0 + 1, 8), :] = across_y1
         fz[pl.ds(x0, 8), pl.ds(y0, 8), :] = up
+        if not frame:
+            inverse = recip(at(w, x0, y0) + faces)
+            w[pl.ds(x0, 8), pl.ds(y0, 8), :] = inverse
+            b[pl.ds(x0, 8), pl.ds(y0, 8), :] = inverse * at(r, x0, y0)
+
+    def weights(x0, y0):
+        faces = at(c, x0, y0)
+        inverse = jnp.where(faces >= 0.0, recip(at(w, x0, y0) + jnp.maximum(faces, 0.0)), 0.0)
         w[pl.ds(x0, 8), pl.ds(y0, 8), :] = inverse
         b[pl.ds(x0, 8), pl.ds(y0, 8), :] = inverse * at(r, x0, y0)
 
@@ -223,9 +229,9 @@
         def column(j):
             for i in range(x_low, x_high):
                 body(1 + 8 * i, 4 + 8 * j)
-        loop(y_low, y_high, column, 1)
-
-    def ring(body, depth, unroll):
+        loop(y_low, y_high, column, 2)
+
+    def ring(body, depth, unroll, between=lambda: None):
         low_y, high_y = depth, nby - 1 - depth
         low_x, high_x = depth, nbx - 1 - depth
 
@@ -233,6 +239,7 @@
             body(1 + 8 * low_x, 4 + 8 * j)
             body(1 + 8 * high_x, 4 + 8 * j)
         loop(low_y, high_y + 1, along_y, unroll)
+        between()
 
         def along_x(i):
             body(1 + 8 * i, 4 + 8 * low_y)
@@ -245,8 +252,8 @@
     def inner(body):
         region(body, 2, nbx - 2, 2, nby - 2)
 
-    def frame(body, unroll=4):
-        ring(body, 0, unroll)
+    def frame(body, unroll=4, between=lambda: None):
+        ring(body, 0, unroll, between)
 
     def border(body):
         ring(body, 1, 4)
@@ -301,14 +308,16 @@
     for copy in local:
         copy.wait()
     interior(functools.partial(coefficients, frame=False))
+    wait_recv(halos[:8])
+    frame(functools.partial(coefficients, frame=True), 1)
     inner(second_sweep)
-    wait_recv(halos)
-    frame(functools.partial(coefficients, frame=True), 1)
+    wait_recv(halos[8:])
+    frame(weights)
     frame(second_sweep)
     border(second_sweep)
-    frame(third_frame)
     back = returns(0)
-    start(back)
+    frame(third_frame, 4, lambda: start(back[:2]))
+    start(back[2:])
     interior(third_first)
     wait_recv(back)
     gather_all(0)
@@ -321,18 +330,45 @@
     frame(restart)
     frame(second_sweep)
     border(second_sweep)
-    frame(third_frame)
     back = returns(1)
-    start(back)
+    frame(third_frame, 4, lambda: start(back[:2]))
+    start(back[2:])
     wait_send(spread)
     interior(third_last)
+
+    def store(i, x0, rows, y0, columns):
+        return pltpu.make_async_copy(
+            pr.at[pl.ds(PADX + x0, rows), pl.ds(PADY + y0, columns), :],
+            out.at[pl.ds(x0, rows), pl.ds(y0, columns), :], lsem.at[i])
+
+    middle = store(0, 4, bx - 8, 8, by - 16)
+    edges = [store(1, 0, 4, 0, by), store(2, bx - 4, 4, 0, by),
+             store(3, 4, bx - 8, 0, 8), store(4, 4, bx - 8, by - 8, 8)]
+    middle.start()
     wait_recv(back)
     gather_all(1)
-    final = pltpu.make_async_copy(pr.at[own_x, own_y, :], out, lsem.at[0])
-    final.start()
+    for copy in edges:
+        copy.start()
     wait_send(halos)
     wait_send(back)
-    final.wait()
+    for copy in (*edges, middle):
+        copy.wait()
+
+
+def relay(source, target, held, sem):
+    rows = source.shape[0] // 8
+    spans = [pl.ds(i * rows, rows) for i in range(8)]
+    reads = [pltpu.make_async_copy(source.at[span], held.at[span], sem.at[0, i])
+             for i, span in enumerate(spans)]
+    writes = [pltpu.make_async_copy(held.at[span], target.at[span], sem.at[1, i])
+              for i, span in enumerate(spans)]
+    for copy in reads:
+        copy.start()
+    for read, write in zip(reads, writes):
+        read.wait()
+        write.start()
+    for copy in writes:
+        copy.wait()
 
 
 def shards(n_sub, n_col, perm, accum, rhs, depth_x, depth_y):
@@ -342,7 +378,7 @@
     hbm = pl.BlockSpec(memory_space=pl.ANY)
     vmem = pl.BlockSpec(memory_space=pltpu.VMEM)
     copies = 16 + 4 + 8 + 4
-    return pl.pallas_call(
+    result = pl.pallas_call(
         functools.partial(kernel, n_sub, n_col, bx, by),
         out_shape=jax.ShapeDtypeStruct((bx, by, nz), jnp.float32),
         in_specs=[hbm, hbm, hbm, vmem, vmem],
@@ -356,13 +392,20 @@
             pltpu.VMEM((2, 2, bx, 8, nz), jnp.float32),
             pltpu.SemaphoreType.DMA((copies,)),
             pltpu.SemaphoreType.DMA((copies,)),
-            pltpu.SemaphoreType.DMA((3,)),
+            pltpu.SemaphoreType.DMA((5,)),
         ],
         compiler_params=pltpu.CompilerParams(
             collective_id=0, has_side_effects=True, vmem_limit_bytes=60 * 1024 * 1024),
         cost_estimate=pl.CostEstimate(
             flops=120 * bx * by * nz, bytes_accessed=16 * bx * by * nz, transcendentals=0),
     )(perm, accum, rhs, depth_x, depth_y)
+    return pl.pallas_call(
+        relay,
+        out_shape=jax.ShapeDtypeStruct((bx, by, nz), jnp.float32),
+        in_specs=[hbm], out_specs=hbm,
+        scratch_shapes=[pltpu.VMEM((bx, by, nz), jnp.float32), pltpu.SemaphoreType.DMA((2, 8))],
+        compiler_params=pltpu.CompilerParams(vmem_limit_bytes=16 * 1024 * 1024),
+    )(result)
 
 
 def solution(mesh):

time: 69.3 us -> 63.7 us (0.919)
  Pallas kernels: 62.4 us -> 59.2 us
  local copies, waits for them, and re-layouts: 6.08 us -> 3.56 us
    pallas_call x1, Pallas kernels: 62.4 us -> 56.8 us  [shards(): pl.pallas_call(functools.partial(kernel, n_sub, n_col, bx, by), out_shape...]
    unnamed x2 -> x3, local copies, waits for them, and re-layouts: 6.08 us -> 3.56 us
    pallas_call x0 -> x1, Pallas kernels: none -> 2.42 us  [shards(): pl.pallas_call(relay, out_shape=jax.ShapeDtypeStruct((bx, by, nz), jnp.fl...]
where the time goes in v3:
time: 63.7 us; the launch traced here: 62.8 us
  Pallas kernels  59.2 us (93%)
  local copies, waits for them, and re-layouts  3.56 us (6%)
    pallas_call x1, Pallas kernels, shards(): pl.pallas_call(functools.partial(kernel, n_sub, n_col, bx, by), out_shape...  56.8 us
    unnamed x3, local copies, waits for them, and re-layouts  3.56 us
    pallas_call x1, Pallas kernels, shards(): pl.pallas_call(relay, out_shape=jax.ShapeDtypeStruct((bx, by, nz), jnp.fl...  2.42 us

profile of v3, /device:TPU:4, one launch (start us, length us, event | category | flops | bytes accessed | tf_op | source)
XLA Modules:
  0.0 62.8 jit_solution(15857846020128224135)
XLA Ops:
  0.0 1.4 %copy.6.depth_y = s32[64,2]{1,0:T(8,128)} copy(s32[64,2]{0,1:T(2,128)} %param.9) | data formatting | bytes 1024 | tf_op args[4]
  1.4 56.8 %shard_map.55.source = f32[64,128,128]{2,1,0:T(8,128)} custom-call(f32[64,128,128]{2,1,0:T(8,128)} %perm.1, f32[64,128,128]{2,1,0:T(8,128)} %accum.1, f32[64,128,128]{2,1,0:T(8,128)} %rhs.1, s32[2,128]{1,0:T(2,128)} %depth_x.1, s32[64,2]{1,0:T(8,128)} %copy.6.depth_y), custom_call_target="tpu_custom_call" | custom-call | flops 125829120 | bytes 16777216 | tf_op jit(solution)/shard_map/pallas_call | solution.py:381
  58.2 0.0 copy-start
  58.2 2.2 %copy-done = f32[64,128,128]{2,1,0:T(8,128)S(1)} copy-done((f32[64,128,128]{2,1,0:T(8,128)S(1)}, f32[64,128,128]{2,1,0:T(8,128)}, u32[]{:S(2)}) %copy-start) | copy-done | bytes 4194328
  60.3 2.4 %shard_map.56 = f32[64,128,128]{2,1,0:T(8,128)} custom-call(f32[64,128,128]{2,1,0:T(8,128)S(1)} %copy-done), custom_call_target="tpu_custom_call" | custom-call | tf_op jit(solution)/shard_map/pallas_call | solution.py:402
Async XLA Ops:
  58.2 2.2 %copy-start = (f32[64,128,128]{2,1,0:T(8,128)S(1)}, f32[64,128,128]{2,1,0:T(8,128)}, u32[]{:S(2)}) copy-start(f32[64,128,128]{2,1,0:T(8,128)} %shard_map.55.source) | copy-start | bytes 12582916
